TPU v7x, 256 devices: a whole 4x4x8 slice. The times are simulated.
256 devices in a mesh: grp: 8 (over x, core), dev: 32 (over y, z).
Axes of the slice: x: 4, y: 4, z: 8, core: 2. Of those that a mesh axis runs over, the one named last changes fastest.
Arguments:
- tracer: float32 [96, 1048576], P(None, ('grp', 'dev')), may hold values from 0.05 to 2
- tile_rows: int32 [40960], P(('grp', 'dev')), may hold values from 0 to 8191, as said below
- tile_cols: int32 [40960], P(('grp', 'dev')), may hold values from 0 to 8191, as said below
- tile_values: bfloat16 [40960, 128, 128], P(('grp', 'dev')), may hold values from -0.25 to 0.25
- level_counts: int32 [32768], P(('grp', 'dev')), may hold values from 1 to 32, as said below
- column_owner: int32 [32768], P(('grp', 'dev')), may hold values from 0 to 31, as said below
- half_saturation: float32 [16], replicated, may hold values from 0.1 to 1
- growth_rate: float32 [64], replicated, may hold values from 0.2 to 2
- uptake: float32 [64, 16], replicated, may hold values from 0 to 0.125
- graze_preference: float32 [64, 64], replicated, may hold values from 0 to 0.03125
- graze_maximum: float32 [64], replicated, may hold values from 0.2 to 2
Outputs:
- updated: float32 [96, 1048576], P(None, ('grp', 'dev'))
- production: float32 [32768], P(('grp', 'dev'))
Inputs may be any that keep to these rules, and one draw needn't show every extreme that they name: `tile_rows`: each device holds 160 tiles; taken device after device along dev, the tiles of a group run in increasing row block. Device d of the whole chain of devices owns row blocks d * 32 to d * 32 + 31; its tiles have row blocks of its own or, among its first 20 tiles only, of the device before it in its group. Device 1 of every group holds exactly 20 tiles of device 0's row blocks. `tile_cols`: A tile's column block lies within 16 blocks of its row block, and within the blocks owned by the device that holds the tile and its two neighbours in the chain. `level_counts`: every device's first column has 32 wet levels, its second one 1. `column_owner`: every device sends exactly 4 of its columns to each device of its group.
All inputs are finite; a program needn't handle non-finite values.
Results may differ from a plain program's by a relative error of at most 0.0018.
Values may be sent and summed in bfloat16 or wider, within the bound.
A program may use at most 64 MiB of HBM per device.

v0:
```python
import jax
import jax.numpy as jnp
from jax import lax
from jax.sharding import PartitionSpec as P

NUT = 16
PLK = 64
LEV = 32


highest = lax.Precision.HIGHEST
WATER_DECAY = 0.03
SHADE_DECAY = 0.05
EFFICIENCY = 0.3
MORTALITY = 0.1
REMINERAL = 0.2
TIMESTEP = 0.5


def with_halo(x, sides, width):
    for axis, dim in sides:
        count, length = (lax.axis_size(axis), x.shape[dim])
        up = [(i, (i + 1) % count) for i in range(count - 1)]
        down = [(j, i) for i, j in up]
        last = lax.slice_in_dim(x, length - width, length, axis=dim)
        initial = lax.slice_in_dim(x, 0, width, axis=dim)
        before = lax.ppermute(last, axis, up)
        after = lax.ppermute(initial, axis, down)
        x = jnp.concatenate([before, x, after], axis=dim)
    return x


def from_behind(value, axis, steps):
    count = lax.axis_size(axis)
    initial, last = (max(0, -steps), min(count, count - steps))
    return lax.ppermute(value, axis, [(source, source + steps) for source in range(initial, last)])


def ecosystem(cells, levels, half_saturation, growth_rate, uptake, graze_preference, graze_maximum):
    column_count = levels.shape[0]
    depth_index = lax.broadcasted_iota(jnp.int32, (column_count, LEV), 1).astype(jnp.float32)
    wet_mask = (depth_index < levels[:, None]).astype(jnp.float32).reshape(1, column_count * LEV)
    nutrient = cells[:NUT]
    plankton = cells[NUT : NUT + PLK]
    detritus = cells[NUT + PLK :]
    chlorophyll = (jnp.sum(plankton, axis=0, keepdims=True) / PLK * wet_mask).reshape(
        column_count, LEV
    )
    above_mask = (
        lax.broadcasted_iota(jnp.int32, (LEV, LEV), 0)
        < lax.broadcasted_iota(jnp.int32, (LEV, LEV), 1)
    ).astype(jnp.float32)
    shading = jnp.dot(chlorophyll, above_mask, precision=highest).reshape(1, column_count * LEV)
    sunlight = jnp.exp(
        -WATER_DECAY * depth_index.reshape(1, column_count * LEV) - SHADE_DECAY * shading
    )
    monod_term = nutrient / (nutrient + half_saturation[:, None])
    limitation = jnp.dot(uptake, monod_term, precision=highest)
    capacity = growth_rate[:, None] * sunlight * plankton
    growth = capacity * limitation
    food_sum = jnp.dot(graze_preference, plankton, precision=highest)
    graze_rate = graze_maximum[:, None] * plankton / (1.0 + food_sum)
    grazed = plankton * jnp.dot(graze_preference.T, graze_rate, precision=highest)
    eaten_total = graze_rate * food_sum
    d_plankton = growth - grazed + EFFICIENCY * eaten_total - MORTALITY * plankton
    d_nutrient = -monod_term * jnp.dot(uptake.T, capacity, precision=highest) + REMINERAL * detritus
    waste_flux = ((1.0 - EFFICIENCY) * eaten_total + MORTALITY * plankton).reshape(
        NUT, PLK // NUT, column_count * LEV
    )
    d_detritus = jnp.sum(waste_flux, axis=1) - REMINERAL * detritus
    source = jnp.concatenate([d_nutrient, d_plankton, d_detritus], axis=0) * wet_mask
    column_sum = jnp.sum(
        (jnp.sum(growth, axis=0) / PLK * wet_mask[0]).reshape(column_count, LEV), axis=1
    )
    return (source, column_sum)


def per_device(
    tracer,
    tile_rows,
    tile_cols,
    tile_values,
    level_counts,
    column_owner,
    half_saturation,
    growth_rate,
    uptake,
    graze_preference,
    graze_maximum,
):
    channels, cell_count = tracer.shape
    block_size = tile_values.shape[1]
    block_count = cell_count // block_size
    position = lax.axis_index("grp") * lax.axis_size("dev") + lax.axis_index("dev")
    coarse = tracer.astype(jnp.bfloat16)
    extended = with_halo(coarse, ((("grp", "dev"), 1),), cell_count)
    ext_blocks = extended.reshape(channels, 3 * block_count, block_size)
    window_start = (position - 1) * block_count
    local_block = jnp.clip(tile_cols - window_start, 0, 3 * block_count - 1)
    picked = jnp.take(ext_blocks, local_block, axis=1)
    contrib = jnp.einsum("ctb,tab->tca", picked, tile_values, preferred_element_type=jnp.float32)
    row_slot = tile_rows - window_start
    onehot = (row_slot[:, None] == jnp.arange(2 * block_count)[None, :]).astype(jnp.float32)
    window = jnp.einsum("tw,tca->cwa", onehot, contrib, precision=highest).reshape(
        channels, 2 * cell_count
    )
    passed = from_behind(window[:, :cell_count].astype(jnp.bfloat16), "dev", -1).astype(jnp.float32)
    transport = window[:, cell_count:] + passed
    send_order = jnp.argsort(column_owner, stable=True)
    source, local_sums = ecosystem(
        tracer,
        level_counts.astype(jnp.float32),
        half_saturation,
        growth_rate,
        uptake,
        graze_preference,
        graze_maximum,
    )
    production = lax.all_to_all(
        local_sums[send_order], "dev", split_axis=0, concat_axis=0, tiled=True
    )
    updated = tracer + transport + TIMESTEP * source
    return (updated, production)


def solution(mesh):
    return jax.shard_map(
        per_device,
        mesh=mesh,
        in_specs=(
            P(None, ("grp", "dev")),
            P(("grp", "dev")),
            P(("grp", "dev")),
            P(("grp", "dev"), None, None),
            P(("grp", "dev")),
            P(("grp", "dev")),
            P(),
            P(),
            P(),
            P(),
            P(),
        ),
        out_specs=(P(None, ("grp", "dev")), P(("grp", "dev"))),
        check_vma=False,
    )
```

profile of v0, /device:TPU:2, one launch (start us, length us, event | category | flops | bytes accessed | tf_op | source)
XLA Modules:
  0.0 83.6 jit_solution(8171096333080287472)
XLA Ops:
  0.7 1.6 %convert_element_type.33 = bf16[96,4096]{1,0:T(8,128)(2,1)S(1)} convert(f32[96,4096]{1,0:T(8,128)} %param.11) | non-fusion elementwise | flops 393216 | bytes 2359296 | tf_op jit(solution)/shard_map/convert_element_type | solution.py:95
  2.3 3.8 %collective-permute-start = (bf16[96,4096]{1,0:T(8,128)(2,1)S(1)}, bf16[96,4096]{1,0:T(8,128)(2,1)}, u32[]{:S(2)}, u32[]{:S(2)}) collective-permute-start(bf16[96,4096]{1,0:T(8,128)(2,1)S(1)} %convert_element_type.33), channel_id=1, source_target_pairs={{0,1},{1,2},{2,3},{3,4},{4,5},{5,6},{6,7},{7,8},{8,9},{9,10},{10,1... | collective-permute-start | bytes 2359304 | tf_op jit(solution)/shard_map/ppermute | solution.py:27
  6.1 7.7 %collective-permute-start.1 = (bf16[96,4096]{1,0:T(8,128)(2,1)S(1)}, bf16[96,4096]{1,0:T(8,128)(2,1)}, u32[]{:S(2)}, u32[]{:S(2)}) collective-permute-start(bf16[96,4096]{1,0:T(8,128)(2,1)S(1)} %convert_element_type.33), channel_id=1, source_target_pairs={{1,0},{2,1},{3,2},{4,3},{5,4},{6,5},{7,6},{8,7},{9,8},{10,9},{11,1... | collective-permute-start | bytes 2359304 | tf_op jit(solution)/shard_map/ppermute | solution.py:28
  14.0 2.6 %slice_reduce_fusion = (f32[4096]{0:T(1024)S(1)}, f32[64,4096]{1,0:T(8,128)}, f32[64,4096]{1,0:T(8,128)}) fusion(f32[96,4096]{1,0:T(8,128)S(1)} %copy-done.1, f32[64]{0:T(128)S(1)} %copy-done.11, f32[64,64]{1,0:T(8,128)S(1)} %copy-done), kind=kOutput, calls=%fused_computation.39 | convolution fusion | flops 203419648 | bytes 4243968 | tf_op jit(solution)/shard_map/dot_general | solution.py:61
  16.7 0.3 fusion.18
  17.0 0.1 copy.19
  17.1 0.1 exp.12
  17.2 2.1 %fusion.39 = (f32[4096]{0:T(1024)S(1)}, f32[64,4096]{1,0:T(8,128)}) fusion(f32[64,16]{0,1:T(8,128)S(1)} %copy-done.6, f32[96,4096]{1,0:T(8,128)S(1)} %copy-done.1, f32[16]{0:T(128)S(1)} %copy-done.9, f32[4096]{0:T(1024)S(1)} %exp.12, f32[64]{0:T(128)S(1)} %copy-done.10), kind=kOutput, calls=%fused_computation.71 | convolution fusion | flops 51507200 | bytes 2401280 | tf_op jit(solution)/shard_map/dot_general | solution.py:58
  19.4 0.2 fusion.29
  19.6 2.5 %sort.17 = (s32[128]{0:T(128)}, s32[128]{0:T(128)S(1)}) sort(s32[128]{0:T(128)S(1)} %copy-done.8, s32[128]{0:T(128)S(1)} %iota.33), dimensions={0}, to_apply=%region_4.5 | sort | flops 896 | bytes 2048 | tf_op jit(solution)/shard_map/jit(argsort)/sort | solution.py:109
  22.2 1.2 %gather_fusion.1 = f32[128]{0:T(128)S(1)} fusion(f32[128]{0:T(128)S(1)} %fusion.29, s32[1024]{0:T(1024)S(1)} %pad_clamp_fusion), kind=kCustom, calls=%fused_computation.1 | custom fusion | bytes 1536 | tf_op jit(solution)/shard_map/gather | solution.py:120
  23.4 0.7 all_to_all.8
  24.1 7.2 %all-to-all-start = ((f32[32,4,1]{1,2,0:T(1,128)}), f32[32,4,1]{1,2,0:T(1,128)S(1)}, u32[]{:S(2)}, u32[]{:S(2)}) async-start(f32[32,4,1]{1,2,0:T(1,128)} %bitcast.6), calls=%async_computation | async-start | bytes 32768 | tf_op jit(solution)/shard_map/all_to_all | solution.py:119
  31.3 1.5 %reshape.89 = f32[16,4,4096]{2,1,0:T(4,128)S(1)} reshape(f32[64,4096]{1,0:T(8,128)} %get-tuple-element.7) | data formatting | bytes 2097152 | tf_op jit(solution)/shard_map/reshape | solution.py:67
  32.9 1.4 %reduce_sum.37 = f32[16,4096]{1,0:T(8,128)} reduce(f32[16,4,4096]{2,1,0:T(4,128)S(1)} %reshape.89, f32[]{:T(128)} %constant.18.clone.1), dimensions={1}, to_apply=%region_1.2 | reduce | flops 196608 | bytes 1310724 | tf_op jit(solution)/shard_map/reduce_sum | solution.py:70
  34.2 1.7 %fusion.28 = f32[16,4096]{1,0:T(8,128)} fusion(f32[16,4096]{1,0:T(8,128)} %reduce_sum.37, f32[96,4096]{1,0:T(8,128)S(1)} %copy-done.1), kind=kLoop, calls=%fused_computation.46 | loop fusion | flops 131072 | bytes 786432 | tf_op jit(solution)/shard_map/sub | solution.py:70
  35.9 1.8 %copy_bitcast_fusion.1 = bf16[96,96,128]{2,0,1:T(8,128)(2,1)S(1)} fusion(bf16[96,4096]{1,0:T(8,128)(2,1)} %collective-permute-done.1, bf16[96,4096]{1,0:T(8,128)(2,1)S(1)} %convert_element_type.33, bf16[96,4096]{1,0:T(8,128)(2,1)} %collective-permute-done), kind=kLoop, calls=%fused_computation.19 | loop fusion | flops 7077888 | bytes 4718592 | tf_op jit(solution)/shard_map/reshape | solution.py:97
  37.7 3.2 %gather_fusion = bf16[160,96,128]{2,1,0:T(8,128)(2,1)} fusion(bf16[96,96,128]{2,0,1:T(8,128)(2,1)S(1)} %copy_bitcast_fusion.1, s32[1024]{0:T(1024)S(1)} %pad_clamp_fusion.1), kind=kCustom, calls=%fused_computation | custom fusion | bytes 7864960 | tf_op jit(solution)/shard_map/jit(_take)/gather | solution.py:100
  40.9 7.5 %fusion.9 = f32[160,96,128]{2,1,0:T(8,128)S(1)} fusion(bf16[160,128,128]{2,1,0:T(8,128)(2,1)} %param.14, bf16[160,96,128]{2,1,0:T(8,128)(2,1)} %gather_fusion, pred[160]{0:T(512)(128)(4,1)S(1)} %get-tuple-element.4), kind=kOutput, calls=%fused_computation.14 | convolution fusion | flops 505282560 | bytes 17039520 | tf_op jit(solution)/shard_map/ctb,tab->tca/dot_general | solution.py:101
  48.4 7.9 %fusion = f32[96,128,64]{1,2,0:T(8,128)S(1)} fusion(f32[160,96,128]{2,1,0:T(8,128)S(1)} %fusion.9, s32[160]{0:T(256)S(1)} %broadcast_subtract_fusion), kind=kOutput, calls=%fused_computation.2 | convolution fusion | flops 1509959680 | bytes 11010688 | tf_op jit(solution)/shard_map/tw,tca->cwa/dot_general | solution.py:104
  56.3 2.2 %copy.27 = f32[12,8,64,128]{3,1,2,0:T(8,128)S(1)} copy(f32[12,8,64,128]{3,2,1,0:T(8,128)S(1)} %bitcast.43) | data formatting | bytes 6291456
  58.5 1.0 %slice.55 = bf16[96,4096]{1,0:T(8,128)(2,1)} slice(f32[96,8192]{1,0:T(8,128)S(1)} %bitcast.44), slice={[0:96], [0:4096]} | slice | bytes 1572864 | tf_op jit(solution)/shard_map/slice | solution.py:107
  59.4 1.3 %collective-permute-start.2 = (bf16[96,4096]{1,0:T(8,128)(2,1)}, bf16[96,4096]{1,0:T(8,128)(2,1)}, u32[]{:S(2)}, u32[]{:S(2)}) collective-permute-start(bf16[96,4096]{1,0:T(8,128)(2,1)} %slice.55), channel_id=1, source_target_pairs={{1,0},{2,1},{3,2},{4,3},{5,4},{6,5},{7,6},{8,7},{9,8},{10,9},{11,1... | collective-permute-start | bytes 2359304 | tf_op jit(solution)/shard_map/ppermute | solution.py:36
  60.7 1.5 %fusion.8 = f32[16,4096]{1,0:T(8,128)} fusion(f32[64,16]{0,1:T(8,128)S(1)} %copy-done.6, f32[96,4096]{1,0:T(8,128)S(1)} %copy-done.2, f32[4096]{0:T(1024)S(1)} %exp.12, f32[64]{0:T(128)S(1)} %copy-done.10, f32[16]{0:T(128)S(1)} %copy-done.9), kind=kOutput, calls=%fused_computation.13 | convolution fusion | flops 51249152 | bytes 1855808 | tf_op jit(solution)/shard_map/dot_general | solution.py:66
  62.3 2.7 %fusion.6 = f32[64,4096]{1,0:T(8,128)} fusion(f32[64,4096]{1,0:T(8,128)S(1)} %copy-done.12, f32[64,64]{1,0:T(8,128)S(1)} %copy-done, f32[64,4096]{1,0:T(8,128)S(1)} %copy-done.13, f32[96,4096]{1,0:T(8,128)S(1)} %copy-done.2, f32[64]{0:T(128)S(1)} %copy-done.11), kind=kOutput, calls=%fused_computation.10 | convolution fusion | flops 204734464 | bytes 6325248 | tf_op jit(solution)/shard_map/dot_general | solution.py:63
  64.9 0.1 compare_convert_fusion
  65.0 0.1 reshape.90
  65.1 0.5 broadcast.86
  65.6 0.7 reduce.3
  66.3 0.6 all_to_all.10
  66.9 13.1 %collective-permute-done.2 = bf16[96,4096]{1,0:T(8,128)(2,1)} collective-permute-done((bf16[96,4096]{1,0:T(8,128)(2,1)}, bf16[96,4096]{1,0:T(8,128)(2,1)}, u32[]{:S(2)}, u32[]{:S(2)}) %collective-permute-start.2) | collective-permute-done | bytes 786464 | tf_op jit(solution)/shard_map/ppermute | solution.py:36
  80.1 3.5 %fusion.15 = f32[96,4096]{1,0:T(8,128)} fusion(f32[96,4096]{1,0:T(8,128)} %param.11, f32[96,8192]{1,0:T(8,128)S(1)} %bitcast.45, f32[16,4096]{1,0:T(8,128)S(1)} %copy-done.3, f32[64,4096]{1,0:T(8,128)} %fusion.6, f32[16,4096]{1,0:T(8,128)} %fusion.8, bf16[96,4096]{1,0:T(8,128)(2,1)} %collective-permute-done.2, f32[4096]{0:T(1024)S(1)} %reshape.90), kind=kLoop, calls=%fused_computation.25 | loop fusion | flops 3145728 | bytes 7094272 | tf_op jit(solution)/shard_map/add | solution.py:122
  (44 shorter events, 0.3 us)
Async XLA Ops:
  0.6 13.2 %copy-start = (f32[64,64]{1,0:T(8,128)S(1)}, f32[64,64]{1,0:T(8,128)}, u32[]{:S(2)}) copy-start(f32[64,64]{1,0:T(8,128)} %param.20) | copy-start | bytes 49156
  0.6 13.2 %copy-start.1 = (f32[96,4096]{1,0:T(8,128)S(1)}, f32[96,4096]{1,0:T(8,128)}, u32[]{:S(2)}) copy-start(f32[96,4096]{1,0:T(8,128)} %param.11) | copy-start | bytes 4718596
  0.7 13.2 %copy-start.11 = (f32[64]{0:T(128)S(1)}, f32[64]{0:T(128)}, u32[]{:S(2)}) copy-start(f32[64]{0:T(128)} %param.21) | copy-start | bytes 772
  2.3 33.7 %collective-permute-start = (bf16[96,4096]{1,0:T(8,128)(2,1)S(1)}, bf16[96,4096]{1,0:T(8,128)(2,1)}, u32[]{:S(2)}, u32[]{:S(2)}) collective-permute-start(bf16[96,4096]{1,0:T(8,128)(2,1)S(1)} %convert_element_type.33), channel_id=1, source_target_pairs={{0,1},{1,2},{2,3},{3,4},{4,5},{5,6},{6,7},{7,8},{8,9},{9,10},{10,1... | collective-permute-start | bytes 2359304 | tf_op jit(solution)/shard_map/ppermute | solution.py:27
  6.1 29.8 %collective-permute-start.1 = (bf16[96,4096]{1,0:T(8,128)(2,1)S(1)}, bf16[96,4096]{1,0:T(8,128)(2,1)}, u32[]{:S(2)}, u32[]{:S(2)}) collective-permute-start(bf16[96,4096]{1,0:T(8,128)(2,1)S(1)} %convert_element_type.33), channel_id=1, source_target_pairs={{1,0},{2,1},{3,2},{4,3},{5,4},{6,5},{7,6},{8,7},{9,8},{10,9},{11,1... | collective-permute-start | bytes 2359304 | tf_op jit(solution)/shard_map/ppermute | solution.py:28
  13.9 2.8 %copy-start.7 = (s32[128]{0:T(128)S(1)}, s32[128]{0:T(128)}, u32[]{:S(2)}) copy-start(s32[128]{0:T(128)} %param.15) | copy-start | bytes 1540
  13.9 3.2 %copy-start.6 = (f32[64,16]{0,1:T(8,128)S(1)}, f32[64,16]{0,1:T(8,128)}, u32[]{:S(2)}) copy-start(f32[64,16]{0,1:T(8,128)} %param.19) | copy-start | bytes 12292
  13.9 3.2 %copy-start.9 = (f32[16]{0:T(128)S(1)}, f32[16]{0:T(128)}, u32[]{:S(2)}) copy-start(f32[16]{0:T(128)} %param.17) | copy-start | bytes 196
  13.9 3.2 %copy-start.10 = (f32[64]{0:T(128)S(1)}, f32[64]{0:T(128)}, u32[]{:S(2)}) copy-start(f32[64]{0:T(128)} %param.18) | copy-start | bytes 772
  16.6 3.0 %copy-start.8 = (s32[128]{0:T(128)S(1)}, s32[128]{0:T(128)}, u32[]{:S(2)}) copy-start(s32[128]{0:T(128)} %param.16) | copy-start | bytes 1540
  16.6 14.7 %copy-start.4 = (s32[160]{0:T(256)S(1)}, s32[160]{0:T(256)}, u32[]{:S(2)}) copy-start(s32[160]{0:T(256)} %param.13) | copy-start | bytes 1924
  16.6 14.7 %copy-start.5 = (s32[160]{0:T(256)S(1)}, s32[160]{0:T(256)}, u32[]{:S(2)}) copy-start(s32[160]{0:T(256)} %param.12) | copy-start | bytes 1924
  24.1 41.0 %all-to-all-start = ((f32[32,4,1]{1,2,0:T(1,128)}), f32[32,4,1]{1,2,0:T(1,128)S(1)}, u32[]{:S(2)}, u32[]{:S(2)}) async-start(f32[32,4,1]{1,2,0:T(1,128)} %bitcast.6), calls=%async_computation | async-start | bytes 32768 | tf_op jit(solution)/shard_map/all_to_all | solution.py:119
  56.2 4.5 %copy-start.2 = (f32[96,4096]{1,0:T(8,128)S(1)}, f32[96,4096]{1,0:T(8,128)}, u32[]{:S(2)}) copy-start(f32[96,4096]{1,0:T(8,128)} %param.11) | copy-start | bytes 4718596
  58.5 3.8 %copy-start.12 = (f32[64,4096]{1,0:T(8,128)S(1)}, f32[64,4096]{1,0:T(8,128)}, u32[]{:S(2)}) copy-start(f32[64,4096]{1,0:T(8,128)} %get-tuple-element.10) | copy-start | bytes 3145732
  58.5 3.8 %copy-start.13 = (f32[64,4096]{1,0:T(8,128)S(1)}, f32[64,4096]{1,0:T(8,128)}, u32[]{:S(2)}) copy-start(f32[64,4096]{1,0:T(8,128)} %get-tuple-element.8) | copy-start | bytes 3145732
  59.4 20.6 %collective-permute-start.2 = (bf16[96,4096]{1,0:T(8,128)(2,1)}, bf16[96,4096]{1,0:T(8,128)(2,1)}, u32[]{:S(2)}, u32[]{:S(2)}) collective-permute-start(bf16[96,4096]{1,0:T(8,128)(2,1)} %slice.55), channel_id=1, source_target_pairs={{1,0},{2,1},{3,2},{4,3},{5,4},{6,5},{7,6},{8,7},{9,8},{10,9},{11,1... | collective-permute-start | bytes 2359304 | tf_op jit(solution)/shard_map/ppermute | solution.py:36
  62.3 17.8 %copy-start.3 = (f32[16,4096]{1,0:T(8,128)S(1)}, f32[16,4096]{1,0:T(8,128)}, u32[]{:S(2)}) copy-start(f32[16,4096]{1,0:T(8,128)} %fusion.28) | copy-start | bytes 786436
where the time goes:
time: 84.1 us; the launch traced here: 83.6 us
  matrix products  24.6 us (29%)
  starting transfers between devices  20 us (24%)
  other arithmetic  13.5 us (16%)
  waiting for transfers between devices  13.1 us (16%)
  local copies, waits for them, and re-layouts  11.4 us (14%)
  between operations  0.97 us (1%)
    ppermute x1, waiting for transfers between devices, from_behind(): lax.ppermute(value, axis, [(source, source + steps) for source in range(i...  13.1 us
    dot_general x1, matrix products, per_device(): jnp.einsum('tw,tca->cwa', onehot, contrib, precision=highest)  7.87 us
    ppermute x1, starting transfers between devices, with_halo(): after = lax.ppermute(initial, axis, down)  7.72 us
    dot_general x1, matrix products, per_device(): jnp.einsum('ctb,tab->tca', picked, tile_values, preferred_element_type=jn...  7.47 us
    all_to_all x1, starting transfers between devices, per_device(): lax.all_to_all(local_sums[send_order], 'dev', split_axis=0, concat_axis=0...  7.17 us
    ppermute x1, starting transfers between devices, with_halo(): before = lax.ppermute(last, axis, up)  3.83 us
    add x1, other arithmetic, per_device(): updated = tracer + transport + TIMESTEP * source  3.51 us
    gather x1, local copies, waits for them, and re-layouts, per_device(): picked = jnp.take(ext_blocks, local_block, axis=1)  3.17 us
  transfers between devices with their start and end apart: 4, of which 1 were waited for; matrix products, arithmetic and copies ran while one was open for 51% of the time, Pallas kernels for 0%

commit v1 on v0

v1 whole, which is shorter than its diff:
```python
import functools

import jax
import jax.numpy as jnp
from jax import lax
from jax.experimental import pallas as pl
from jax.experimental.pallas import tpu as pltpu
from jax.sharding import PartitionSpec as P

MESH = pl.DeviceIdType.MESH
F32 = jnp.float32
BF16 = jnp.bfloat16

NUT = 16
PLK = 64
NTR = 96
LEV = 32
COLS = 128
BLK = 128
BPD = 32
NT = 160
SPILL = 20
REACH = 16
CD = BPD * BLK
NZ = 8
WATER_DECAY = 0.03
SHADE_DECAY = 0.05
EFFICIENCY = 0.3
MORTALITY = 0.1
REMINERAL = 0.2
TIMESTEP = 0.5

TILE_CHUNKS = 5
TILES_SENT = SPILL // TILE_CHUNKS
GROUP = 256
UNROLL = 8
SMALL = 7


def iota(shape, dim):
    return lax.broadcasted_iota(jnp.int32, shape, dim)


def split2(x):
    high = x.astype(BF16)
    return high, (x - high.astype(F32)).astype(BF16)


def split3(x):
    high = x.astype(BF16)
    rest = x - high.astype(F32)
    middle = rest.astype(BF16)
    return high, middle, (rest - middle.astype(F32)).astype(BF16)


def weights3(w):
    high, low = split2(w)
    return jnp.concatenate([high, high, low], axis=1)


def data3(x):
    high, low = split2(x)
    return jnp.concatenate([high, low, high], axis=0)


def matmul(a, b):
    return jnp.dot(a, b, preferred_element_type=F32)


def matmul_nt(a, b):
    return lax.dot_general(a, b, (((1,), (1,)), ((), ())), preferred_element_type=F32)


def column_of(row):
    n = row.shape[1]
    return jnp.sum(jnp.where(iota((n, n), 0) == iota((n, n), 1), row, 0.0), axis=1, keepdims=True)


def kernel(
    n_grp,
    n_dev,
    tracer,
    tile_rows,
    tile_cols,
    tiles,
    levels,
    owner,
    half_saturation,
    growth_rate,
    uptake,
    preference,
    graze_maximum,
    updated,
    production,
    tr,
    ext,
    own_tiles,
    got_tiles,
    runs,
    got_runs,
    levels_v,
    owner_v,
    half_v,
    growth_v,
    uptake_v,
    preference_v,
    maximum_v,
    chl,
    wet,
    sun,
    grown,
    w_limit,
    w_food,
    w_graze,
    w_use,
    to_z,
    from_z,
    to_y,
    from_y,
    got_rows,
    got_cols,
    place,
    got_place,
    tracer_sem,
    tiles_sem,
    small_sem,
    halo_send,
    halo_recv,
    spill_send,
    spill_recv,
    rows_sem,
    z_send,
    z_recv,
    y_send,
    y_recv,
):
    ny = n_dev // NZ
    grp = lax.axis_index("grp")
    dev = lax.axis_index("dev")
    me_y = dev // NZ
    me_z = lax.rem(dev, NZ)
    position = grp * n_dev + dev
    count = n_grp * n_dev
    after = lax.rem(position + 1, count)
    before = lax.rem(position + count - 1, count)
    right = (after // n_dev, lax.rem(after, n_dev))
    left = (before // n_dev, lax.rem(before, n_dev))
    z_peers = [(grp, me_y * NZ + lax.rem(me_z + k, NZ)) for k in range(1, NZ)]
    y_peers = [(grp, lax.rem(me_y + k, ny) * NZ + me_z) for k in range(1, ny)]

    barrier = pltpu.get_barrier_semaphore()
    for peer in [left, right] + z_peers + y_peers:
        pl.semaphore_signal(barrier, inc=1, device_id=peer, device_id_type=MESH)

    load = pltpu.make_async_copy(tracer, tr, tracer_sem)
    load.start()
    small = [
        pltpu.make_async_copy(source, target, small_sem.at[i])
        for i, (source, target) in enumerate(
            [
                (levels, levels_v),
                (owner, owner_v),
                (half_saturation, half_v),
                (growth_rate, growth_v),
                (uptake, uptake_v),
                (preference, preference_v),
                (graze_maximum, maximum_v),
            ]
        )
    ]
    for copy in small:
        copy.start()
    load_tiles = pltpu.make_async_copy(tiles, own_tiles, tiles_sem)
    load_tiles.start()

    load.wait()
    for b in range(BPD):
        ext[REACH + b] = tr[:, b * BLK : (b + 1) * BLK].astype(BF16)

    pl.semaphore_wait(barrier, 2 + (NZ - 1) + (ny - 1))

    def remote(source, target, send, recv, peer):
        return pltpu.make_async_remote_copy(
            src_ref=source,
            dst_ref=target,
            send_sem=send,
            recv_sem=recv,
            device_id=peer,
            device_id_type=MESH,
        )

    index_copies = [
        remote(tile_rows, got_rows, rows_sem.at[0], rows_sem.at[1], left),
        remote(tile_cols, got_cols, rows_sem.at[2], rows_sem.at[3], left),
    ]
    halo = [
        remote(
            ext.at[pl.ds(REACH, REACH)],
            ext.at[pl.ds(REACH + BPD, REACH)],
            halo_send.at[0],
            halo_recv.at[0],
            left,
        ),
        remote(
            ext.at[pl.ds(BPD, REACH)],
            ext.at[pl.ds(0, REACH)],
            halo_send.at[1],
            halo_recv.at[1],
            right,
        ),
    ]
    spill = [
        remote(
            tiles.at[pl.ds(c * TILES_SENT, TILES_SENT)],
            got_tiles.at[pl.ds(c * TILES_SENT, TILES_SENT)],
            spill_send.at[c],
            spill_recv.at[c],
            left,
        )
        for c in range(TILE_CHUNKS)
    ]
    for copy in halo:
        copy.start()
    for copy in index_copies:
        copy.start()
    for copy in spill:
        copy.start()

    for copy in small:
        copy.wait()
    w_limit[...] = weights3(uptake_v[...])
    w_food[...] = weights3(preference_v[...])
    w_graze[...] = weights3(preference_v[...].T)
    w_use[...] = weights3(uptake_v[...].T)
    half = column_of(half_v[...])
    growth_column = column_of(growth_v[...])
    maximum = column_of(maximum_v[...])

    column_row = iota((BPD, COLS), 1)
    pick_row = (column_row >> 2) == iota((BPD, COLS), 0)
    in_block = ((iota((COLS, BLK), 0) & 3) == (iota((COLS, BLK), 1) >> 5)).astype(BF16)
    level_row = jnp.where(pick_row, levels_v[...].astype(F32), 0.0).astype(BF16)
    wet_levels = matmul(level_row, in_block)
    depth = (iota((BPD, BLK), 1) & (LEV - 1)).astype(F32)
    wet_mask = (depth < wet_levels).astype(F32)
    wet[...] = wet_mask

    def sum_plankton(i, carry):
        lanes = pl.ds(pl.multiple_of(i * BLK, BLK), BLK)
        chl[pl.ds(i, 1), :] = jnp.sum(tr[NUT : NUT + PLK, lanes], axis=0, keepdims=True)
        return carry

    lax.fori_loop(0, BPD, sum_plankton, 0, unroll=4)
    upper_row, upper_col = iota((2 * BLK, BLK), 0) & (BLK - 1), iota((2 * BLK, BLK), 1)
    above = ((upper_row < upper_col) & ((upper_row >> 5) == (upper_col >> 5))).astype(BF16)
    chl_high, chl_low = split2(chl[...] * (1.0 / PLK) * wet_mask)
    shading = matmul(jnp.concatenate([chl_high, chl_low], axis=1), above)
    sun[...] = jnp.exp(-WATER_DECAY * depth - SHADE_DECAY * shading)

    fold_col = iota((NUT, 2 * PLK), 1) & (PLK - 1)
    fold = ((fold_col >> 2) == iota((NUT, 2 * PLK), 0)).astype(BF16)
    per_group = GROUP // BLK

    def row_of(ref, i):
        return jnp.concatenate([ref[pl.ds(i * per_group + h, 1), :] for h in range(per_group)], axis=1)

    def ecosystem(i, carry):
        lanes = pl.ds(pl.multiple_of(i * GROUP, GROUP), GROUP)
        mask = row_of(wet, i) * TIMESTEP
        light = row_of(sun, i)
        nutrient = tr[:NUT, lanes]
        plankton = tr[NUT : NUT + PLK, lanes]
        detritus = tr[NUT + PLK :, lanes]
        monod = nutrient / (nutrient + half)
        limitation = matmul(w_limit[...], data3(monod))
        capacity = growth_column * (light * plankton)
        growth = capacity * limitation
        food = matmul(w_food[...], data3(plankton))
        rate = maximum * plankton / (1.0 + food)
        eaten = rate * food
        grazed = plankton * matmul(w_graze[...], data3(rate))
        mortality = MORTALITY * plankton
        d_plankton = growth - grazed + EFFICIENCY * eaten - mortality
        use = matmul(w_use[...], data3(capacity))
        d_nutrient = REMINERAL * detritus - monod * use
        waste = (1.0 - EFFICIENCY) * eaten + mortality
        d_detritus = matmul(fold, jnp.concatenate(split2(waste), axis=0)) - REMINERAL * detritus
        updated[:NUT, lanes] = nutrient + mask * d_nutrient
        updated[NUT : NUT + PLK, lanes] = plankton + mask * d_plankton
        updated[NUT + PLK :, lanes] = detritus + mask * d_detritus
        total = jnp.sum(growth, axis=0, keepdims=True)
        for h in range(per_group):
            grown[pl.ds(i * per_group + h, 1), :] = total[:, h * BLK : (h + 1) * BLK]
        return carry

    lax.fori_loop(0, CD // GROUP, ecosystem, 0)

    summed = jnp.concatenate(split3(grown[...] * (1.0 / PLK) * wet_mask), axis=1)
    lane_row, lane_col = iota((3 * BLK, COLS), 0) & (BLK - 1), iota((3 * BLK, COLS), 1)
    gather_columns = ((lane_row >> 5) == (lane_col & 3)).astype(BF16)
    by_block = matmul(summed, gather_columns)
    column_sum = jnp.sum(jnp.where(pick_row, by_block, 0.0), axis=0, keepdims=True)
    slot = iota((8 * NZ, COLS), 0)
    slot_owner = (slot & 7) * NZ + (slot >> 3)
    mine = (slot_owner == owner_v[...]) & ((slot & 7) < ny)
    mine_f = mine.astype(F32)
    earlier = (iota((COLS, COLS), 0) < iota((COLS, COLS), 1)).astype(BF16)
    seen = matmul(mine_f.astype(BF16), earlier)
    rank = jnp.sum(mine_f * seen, axis=0, keepdims=True)
    target = rank + (dev * (COLS // n_dev)).astype(F32)
    put = (iota((COLS, COLS), 0).astype(F32) == target).astype(BF16)
    sums = jnp.concatenate(split3(jnp.where(mine, column_sum, 0.0)), axis=1)
    to_z[...] = matmul_nt(sums, jnp.concatenate([put, put, put], axis=1)).reshape(NZ, 8, COLS)
    from_z[me_z] = to_z[me_z]
    z_copies = [
        remote(to_z.at[lax.rem(me_z + k, NZ)], from_z.at[me_z], z_send.at[k], z_recv.at[k], z_peers[k - 1])
        for k in range(1, NZ)
    ]
    for copy in z_copies:
        copy.start()

    first_row = position * BPD

    def find(rows, limit, length, steps, wanted):
        found = jnp.int32(0)
        for step in steps:
            trial = found + step
            at = rows[jnp.minimum(trial, length) - 1]
            found = jnp.where((trial <= length) & (at <= wanted), trial, found)
        last = jnp.maximum(found - 1, 0)
        return last, jnp.where((found > 0) & (rows[last] == wanted), 1, 0)

    def find_own(r, carry):
        last, held = find(tile_rows, NT, NT, (128, 64, 32, 16, 8, 4, 2, 1), first_row + r)
        place[0, r] = last
        place[1, r] = held
        return carry

    lax.fori_loop(0, BPD, find_own, 0)
    for copy in index_copies:
        copy.wait()

    def find_got(r, carry):
        last, held = find(got_rows, SPILL, SPILL, (16, 8, 4, 2, 1), first_row + r)
        got_place[0, r] = last
        got_place[1, r] = held
        return carry

    lax.fori_loop(0, BPD, find_got, 0)

    load_tiles.wait()
    for copy in halo:
        copy.wait()

    first_col = first_row - REACH

    def own(t, run):
        block = jnp.clip(tile_cols[t] - first_col, 0, BPD + 2 * REACH - 1)
        term = matmul_nt(ext[block], own_tiles[t])
        goes_on = tile_rows[t] == tile_rows[jnp.maximum(t - 1, 0)]
        run = jnp.where(goes_on, run, 0.0) + term
        runs[t] = run
        return run

    lax.fori_loop(0, NT, own, jnp.zeros((NTR, BLK), F32), unroll=UNROLL)

    for r in range(BPD):
        lanes = slice(r * BLK, (r + 1) * BLK)
        updated[:, lanes] += jnp.where(place[1, r] == 1, runs[place[0, r]], 0.0)

    for copy in z_copies:
        copy.wait()
    over_z = from_z[0]
    for k in range(1, NZ):
        over_z += from_z[k]
    to_y[...] = over_z
    from_y[me_y] = over_z
    y_copies = [
        remote(to_y, from_y.at[me_y], y_send.at[k], y_recv.at[k], y_peers[k - 1]) for k in range(1, ny)
    ]
    for copy in y_copies:
        copy.start()

    run = jnp.zeros((NTR, BLK), F32)
    for c in range(TILE_CHUNKS):
        spill[c].wait()
        for s in range(c * TILES_SENT, (c + 1) * TILES_SENT):
            block = jnp.clip(got_cols[s] - first_col, 0, BPD + 2 * REACH - 1)
            term = matmul_nt(ext[block], got_tiles[s])
            goes_on = got_rows[s] == got_rows[max(s - 1, 0)]
            run = jnp.where(goes_on, run, 0.0) + term
            got_runs[s] = run

    for r in range(BPD):
        lanes = slice(r * BLK, (r + 1) * BLK)
        updated[:, lanes] += jnp.where(got_place[1, r] == 1, got_runs[got_place[0, r]], 0.0)

    for copy in y_copies:
        copy.wait()
    over_y = from_y[0]
    for k in range(1, ny):
        over_y += from_y[k]
    in_row = iota((8, COLS), 0) == me_y
    production[...] = jnp.sum(jnp.where(in_row, over_y, 0.0), axis=0, keepdims=True)


def per_device(
    n_grp,
    n_dev,
    tracer,
    tile_rows,
    tile_cols,
    tile_values,
    level_counts,
    column_owner,
    half_saturation,
    growth_rate,
    uptake,
    graze_preference,
    graze_maximum,
):
    ny = n_dev // NZ
    anywhere = pl.BlockSpec(memory_space=pl.ANY)
    scalars = pl.BlockSpec(memory_space=pltpu.SMEM)
    vector = pl.BlockSpec(memory_space=pltpu.VMEM)
    dma = pltpu.SemaphoreType.DMA
    updated, production = pl.pallas_call(
        functools.partial(kernel, n_grp, n_dev),
        out_shape=(
            jax.ShapeDtypeStruct((NTR, CD), F32),
            jax.ShapeDtypeStruct((1, COLS), F32),
        ),
        in_specs=[anywhere, scalars, scalars] + [anywhere] * 8,
        out_specs=(vector, vector),
        scratch_shapes=[
            pltpu.VMEM((NTR, CD), F32),
            pltpu.VMEM((BPD + 2 * REACH, NTR, BLK), BF16),
            pltpu.VMEM((NT, BLK, BLK), BF16),
            pltpu.VMEM((SPILL, BLK, BLK), BF16),
            pltpu.VMEM((NT, NTR, BLK), F32),
            pltpu.VMEM((SPILL, NTR, BLK), F32),
            pltpu.VMEM((1, COLS), jnp.int32),
            pltpu.VMEM((1, COLS), jnp.int32),
            pltpu.VMEM((1, NUT), F32),
            pltpu.VMEM((1, PLK), F32),
            pltpu.VMEM((PLK, NUT), F32),
            pltpu.VMEM((PLK, PLK), F32),
            pltpu.VMEM((1, PLK), F32),
            pltpu.VMEM((BPD, BLK), F32),
            pltpu.VMEM((BPD, BLK), F32),
            pltpu.VMEM((BPD, BLK), F32),
            pltpu.VMEM((BPD, BLK), F32),
            pltpu.VMEM((PLK, 3 * NUT), BF16),
            pltpu.VMEM((PLK, 3 * PLK), BF16),
            pltpu.VMEM((PLK, 3 * PLK), BF16),
            pltpu.VMEM((NUT, 3 * PLK), BF16),
            pltpu.VMEM((NZ, 8, COLS), F32),
            pltpu.VMEM((NZ, 8, COLS), F32),
            pltpu.VMEM((8, COLS), F32),
            pltpu.VMEM((ny, 8, COLS), F32),
            pltpu.SMEM((NT,), jnp.int32),
            pltpu.SMEM((NT,), jnp.int32),
            pltpu.SMEM((2, BPD), jnp.int32),
            pltpu.SMEM((2, BPD), jnp.int32),
            dma,
            dma,
            dma((SMALL,)),
            dma((2,)),
            dma((2,)),
            dma((TILE_CHUNKS,)),
            dma((TILE_CHUNKS,)),
            dma((4,)),
            dma((NZ,)),
            dma((NZ,)),
            dma((ny,)),
            dma((ny,)),
        ],
        compiler_params=pltpu.CompilerParams(
            collective_id=0, has_side_effects=True, vmem_limit_bytes=56 * 1024 * 1024
        ),
        name="plankton_step",
    )(
        tracer,
        tile_rows,
        tile_cols,
        tile_values,
        level_counts.reshape(1, COLS),
        column_owner.reshape(1, COLS),
        half_saturation.reshape(1, NUT),
        growth_rate.reshape(1, PLK),
        uptake,
        graze_preference,
        graze_maximum.reshape(1, PLK),
    )
    return updated, production.reshape(COLS)


def solution(mesh):
    n_grp, n_dev = mesh.shape["grp"], mesh.shape["dev"]
    chain = P(("grp", "dev"))
    cells = P(None, ("grp", "dev"))
    return jax.shard_map(
        functools.partial(per_device, n_grp, n_dev),
        mesh=mesh,
        in_specs=(cells, chain, chain, P(("grp", "dev"), None, None), chain, chain, P(), P(), P(), P(), P()),
        out_specs=(cells, chain),
        check_vma=False,
    )
```

time: 84.1 us -> 45.1 us (0.54)
  Pallas kernels: 0 us -> 39.7 us
  matrix products: 24.6 us -> 0 us
  starting transfers between devices: 20 us -> 0 us
  other arithmetic: 13.5 us -> 0 us
  waiting for transfers between devices: 13.1 us -> 0 us
  local copies, waits for them, and re-layouts: 11.4 us -> 4.56 us
    pallas_call x0 -> x1, Pallas kernels: none -> 39.7 us  [per_device(): pl.pallas_call(functools.partial(kernel, n_grp, n_dev), out_shape=(jax.Sh...]
    dot_general x7 -> x0, matrix products: 24.6 us -> none  [the longest x1 7.87 us: per_device(): jnp.einsum('tw,tca->cwa', onehot, contrib, precision=highest)]
    ppermute x3 -> x0, waiting for transfers between devices: 13.1 us -> none  [the longest x1 13.1 us: from_behind(): lax.ppermute(value, axis, [(source, source + steps) for source in range(i...]
    ppermute x3 -> x0, starting transfers between devices: 12.8 us -> none  [the longest x1 7.72 us: with_halo(): after = lax.ppermute(initial, axis, down)]
    all_to_all x1 -> x0, starting transfers between devices: 7.17 us -> none  [per_device(): lax.all_to_all(local_sums[send_order], 'dev', split_axis=0, concat_axis=0...]
    gather x2 -> x0, local copies, waits for them, and re-layouts: 4.39 us -> none  [the longest x1 3.17 us: per_device(): picked = jnp.take(ext_blocks, local_block, axis=1)]
    add x1 -> x0, other arithmetic: 3.51 us -> none  [per_device(): updated = tracer + transport + TIMESTEP * source]
    sort x1 -> x0, other arithmetic: 2.54 us -> none  [per_device(): send_order = jnp.argsort(column_owner, stable=True)]
  transfers between devices with their start and end apart: 4 -> 0, of which waited for: 1 -> 0; matrix products, arithmetic and copies ran while one was open for 51% -> 0% of each run, Pallas kernels for 0% -> 0%
where the time goes in v1:
time: 45.1 us; the launch traced here: 44.9 us
  Pallas kernels  39.7 us (88%)
  local copies, waits for them, and re-layouts  4.56 us (10%)
  between operations  0.65 us (1%)
    pallas_call x1, Pallas kernels, per_device(): pl.pallas_call(functools.partial(kernel, n_grp, n_dev), out_shape=(jax.Sh...  39.7 us
    unnamed x5, local copies, waits for them, and re-layouts  4.56 us

profile of v1, /device:TPU:2, one launch (start us, length us, event | category | flops | bytes accessed | tf_op | source)
XLA Modules:
  0.0 44.9 jit_solution(7161634593335552133)
XLA Ops:
  0.6 1.4 %copy.13.uptake = f32[64,16]{1,0:T(8,128)} copy(f32[64,16]{0,1:T(8,128)} %param.19) | data formatting | bytes 8192 | tf_op args[8]
  2.0 39.7 %plankton_step.1 = (f32[96,4096]{1,0:T(8,128)}, f32[1,128]{1,0:T(1,128)}) custom-call(f32[96,4096]{1,0:T(8,128)} %tracer.1, s32[160]{0:T(256)} %tile_rows.1, s32[160]{0:T(256)} %tile_cols.1, bf16[160,128,128]{2,1,0:T(8,128)(2,1)} %tiles.1, s32[1,128]{1,0:T(1,128)} %bitcast.6, s32[1,128]{1,0:T(1,128)} %bitcast.7, f32[1,16]{1,0:T(1,128)} %bitcast.8, ...), custom_call_target="tpu_custom_call" | custom-call | tf_op jit(solution)/shard_map/plankton_step/pallas_call | solution.py:427
  41.8 0.0 copy-start
  41.8 2.7 %copy.16 = f32[96,4096]{1,0:T(8,128)} copy(f32[96,4096]{1,0:T(8,128)} %get-tuple-element.8) | data formatting | bytes 3145728
  44.4 0.0 copy-done
  44.4 0.5 %copy.17 = f32[128]{0:T(128)} copy(f32[128]{0:T(128)S(1)} %bitcast.11) | data formatting | bytes 1024
Async XLA Ops:
  41.8 2.7 %copy-start = (f32[1,128]{1,0:T(1,128)S(1)}, f32[1,128]{1,0:T(1,128)}, u32[]{:S(2)}) copy-start(f32[1,128]{1,0:T(1,128)} %get-tuple-element.5) | copy-start | bytes 1540

commit v2 on v1

--- a/solution.py
+++ b/solution.py
@@ -173,10 +173,6 @@
     load_tiles = pltpu.make_async_copy(tiles, own_tiles, tiles_sem)
     load_tiles.start()
 
-    load.wait()
-    for b in range(BPD):
-        ext[REACH + b] = tr[:, b * BLK : (b + 1) * BLK].astype(BF16)
-
     pl.semaphore_wait(barrier, 2 + (NZ - 1) + (ny - 1))
 
     def remote(source, target, send, recv, peer):
@@ -211,7 +207,7 @@
     ]
     spill = [
         remote(
-            tiles.at[pl.ds(c * TILES_SENT, TILES_SENT)],
+            (own_tiles if c else tiles).at[pl.ds(c * TILES_SENT, TILES_SENT)],
             got_tiles.at[pl.ds(c * TILES_SENT, TILES_SENT)],
             spill_send.at[c],
             spill_recv.at[c],
@@ -219,19 +215,25 @@
         )
         for c in range(TILE_CHUNKS)
     ]
-    for copy in halo:
-        copy.start()
+    def round_blocks(first, blocks):
+        for b in range(first, first + blocks):
+            ext[REACH + b] = tr[:, b * BLK : (b + 1) * BLK].astype(BF16)
+
+    spill[0].start()
     for copy in index_copies:
         copy.start()
-    for copy in spill:
-        copy.start()
+    load.wait()
+    round_blocks(0, REACH)
+    halo[0].start()
+    round_blocks(REACH, BPD - REACH)
+    halo[1].start()
 
     for copy in small:
         copy.wait()
-    w_limit[...] = weights3(uptake_v[...])
+    w_limit[...] = weights3(uptake_v[...].T)
     w_food[...] = weights3(preference_v[...])
     w_graze[...] = weights3(preference_v[...].T)
-    w_use[...] = weights3(uptake_v[...].T)
+    w_use[...] = weights3(uptake_v[...])
     half = column_of(half_v[...])
     growth_column = column_of(growth_v[...])
     maximum = column_of(maximum_v[...])
@@ -352,6 +354,9 @@
     for copy in halo:
         copy.wait()
 
+    for copy in spill[1:]:
+        copy.start()
+
     first_col = first_row - REACH
 
     def own(t, run):
@@ -401,7 +406,7 @@
     for k in range(1, ny):
         over_y += from_y[k]
     in_row = iota((8, COLS), 0) == me_y
-    production[...] = jnp.sum(jnp.where(in_row, over_y, 0.0), axis=0, keepdims=True)
+    production[...] = jnp.sum(jnp.where(in_row, over_y, 0.0), axis=0)
 
 
 def per_device(
@@ -427,8 +432,8 @@
     updated, production = pl.pallas_call(
         functools.partial(kernel, n_grp, n_dev),
         out_shape=(
-            jax.ShapeDtypeStruct((NTR, CD), F32),
-            jax.ShapeDtypeStruct((1, COLS), F32),
+            pltpu.VMEM((NTR, CD), F32),
+            pltpu.VMEM((COLS,), F32),
         ),
         in_specs=[anywhere, scalars, scalars] + [anywhere] * 8,
         out_specs=(vector, vector),
@@ -443,7 +448,7 @@
             pltpu.VMEM((1, COLS), jnp.int32),
             pltpu.VMEM((1, NUT), F32),
             pltpu.VMEM((1, PLK), F32),
-            pltpu.VMEM((PLK, NUT), F32),
+            pltpu.VMEM((NUT, PLK), F32),
             pltpu.VMEM((PLK, PLK), F32),
             pltpu.VMEM((1, PLK), F32),
             pltpu.VMEM((BPD, BLK), F32),
@@ -488,11 +493,11 @@
         column_owner.reshape(1, COLS),
         half_saturation.reshape(1, NUT),
         growth_rate.reshape(1, PLK),
-        uptake,
+        uptake.T,
         graze_preference,
         graze_maximum.reshape(1, PLK),
     )
-    return updated, production.reshape(COLS)
+    return updated, production
 
 
 def solution(mesh):

time: 45.1 us -> 36.7 us (0.81)
  Pallas kernels: 39.7 us -> 34.3 us
  local copies, waits for them, and re-layouts: 4.56 us -> 1.66 us
    pallas_call x1, Pallas kernels: 39.7 us -> 34.3 us  [per_device(): pl.pallas_call(functools.partial(kernel, n_grp, n_dev), out_shape=(pltpu....]
    unnamed x5 -> x2, local copies, waits for them, and re-layouts: 4.56 us -> 1.66 us
where the time goes in v2:
time: 36.7 us; the launch traced here: 36.6 us
  Pallas kernels  34.3 us (93%)
  local copies, waits for them, and re-layouts  1.66 us (5%)
  between operations  0.64 us (2%)
    pallas_call x1, Pallas kernels, per_device(): pl.pallas_call(functools.partial(kernel, n_grp, n_dev), out_shape=(pltpu....  34.3 us
    unnamed x2, local copies, waits for them, and re-layouts  1.66 us

profile of v2, /device:TPU:2, one launch (start us, length us, event | category | flops | bytes accessed | tf_op | source)
XLA Modules:
  0.0 36.6 jit_solution(14288900841286282061)
XLA Ops:
  0.6 34.3 %plankton_step.1 = (f32[96,4096]{1,0:T(8,128)S(1)}, f32[128]{0:T(128)S(1)}) custom-call(f32[96,4096]{1,0:T(8,128)} %tracer.1, s32[160]{0:T(256)} %tile_rows.1, s32[160]{0:T(256)} %tile_cols.1, bf16[160,128,128]{2,1,0:T(8,128)(2,1)} %tiles.1, s32[1,128]{1,0:T(1,128)} %bitcast.7, s32[1,128]{1,0:T(1,128)} %bitcast.8, f32[1,16]{1,0:T(1,128)} %bitcast.9, ...), custom_call_target="tpu_custom_call" | custom-call | tf_op jit(solution)/shard_map/plankton_step/pallas_call | solution.py:432
  34.9 1.1 %copy.15 = f32[96,4096]{1,0:T(8,128)} copy(f32[96,4096]{1,0:T(8,128)S(1)} %get-tuple-element.2) | data formatting | bytes 3145728
  36.1 0.5 %copy.16 = f32[128]{0:T(128)} copy(f32[128]{0:T(128)S(1)} %get-tuple-element.3) | data formatting | bytes 1024

commit v3 on v2

--- a/solution.py
+++ b/solution.py
@@ -34,7 +34,7 @@
 TILES_SENT = SPILL // TILE_CHUNKS
 GROUP = 256
 UNROLL = 8
-SMALL = 7
+SMALL = 9
 
 
 def iota(shape, dim):
@@ -80,8 +80,8 @@
     n_grp,
     n_dev,
     tracer,
-    tile_rows,
-    tile_cols,
+    rows_in,
+    cols_in,
     tiles,
     levels,
     owner,
@@ -117,6 +117,8 @@
     from_z,
     to_y,
     from_y,
+    tile_rows,
+    tile_cols,
     got_rows,
     got_cols,
     place,
@@ -165,6 +167,8 @@
                 (uptake, uptake_v),
                 (preference, preference_v),
                 (graze_maximum, maximum_v),
+                (rows_in, tile_rows),
+                (cols_in, tile_cols),
             ]
         )
     ]
@@ -186,8 +190,8 @@
         )
 
     index_copies = [
-        remote(tile_rows, got_rows, rows_sem.at[0], rows_sem.at[1], left),
-        remote(tile_cols, got_cols, rows_sem.at[2], rows_sem.at[3], left),
+        remote(rows_in, got_rows, rows_sem.at[0], rows_sem.at[1], left),
+        remote(cols_in, got_cols, rows_sem.at[2], rows_sem.at[3], left),
     ]
     halo = [
         remote(
@@ -219,7 +223,8 @@
         for b in range(first, first + blocks):
             ext[REACH + b] = tr[:, b * BLK : (b + 1) * BLK].astype(BF16)
 
-    spill[0].start()
+    for copy in spill[0:1]:
+        copy.start()
     for copy in index_copies:
         copy.start()
     load.wait()
@@ -321,6 +326,9 @@
     for copy in z_copies:
         copy.start()
 
+    load_tiles.wait()
+    for copy in spill[1:3]:
+        copy.start()
     first_row = position * BPD
 
     def find(rows, limit, length, steps, wanted):
@@ -350,12 +358,10 @@
 
     lax.fori_loop(0, BPD, find_got, 0)
 
-    load_tiles.wait()
-    for copy in halo:
-        copy.wait()
-
-    for copy in spill[1:]:
-        copy.start()
+    halo[0].wait_send()
+
+    halo[0].wait_recv()
+    halo[1].wait()
 
     first_col = first_row - REACH
 
@@ -367,11 +373,7 @@
         runs[t] = run
         return run
 
-    lax.fori_loop(0, NT, own, jnp.zeros((NTR, BLK), F32), unroll=UNROLL)
-
-    for r in range(BPD):
-        lanes = slice(r * BLK, (r + 1) * BLK)
-        updated[:, lanes] += jnp.where(place[1, r] == 1, runs[place[0, r]], 0.0)
+    run = lax.fori_loop(0, 80, own, jnp.zeros((NTR, BLK), F32), unroll=UNROLL)
 
     for copy in z_copies:
         copy.wait()
@@ -386,6 +388,15 @@
     for copy in y_copies:
         copy.start()
 
+    for copy in spill[3:]:
+        copy.start()
+
+    lax.fori_loop(80, NT, own, run, unroll=UNROLL)
+
+    for r in range(BPD):
+        lanes = slice(r * BLK, (r + 1) * BLK)
+        updated[:, lanes] += jnp.where(place[1, r] == 1, runs[place[0, r]], 0.0)
+
     run = jnp.zeros((NTR, BLK), F32)
     for c in range(TILE_CHUNKS):
         spill[c].wait()
@@ -407,6 +418,17 @@
         over_y += from_y[k]
     in_row = iota((8, COLS), 0) == me_y
     production[...] = jnp.sum(jnp.where(in_row, over_y, 0.0), axis=0)
+
+
+def write_out(updated, production, updated_out, production_out, sem):
+    copies = [
+        pltpu.make_async_copy(updated, updated_out, sem.at[0]),
+        pltpu.make_async_copy(production, production_out, sem.at[1]),
+    ]
+    for copy in copies:
+        copy.start()
+    for copy in copies:
+        copy.wait()
 
 
 def per_device(
@@ -426,7 +448,6 @@
 ):
     ny = n_dev // NZ
     anywhere = pl.BlockSpec(memory_space=pl.ANY)
-    scalars = pl.BlockSpec(memory_space=pltpu.SMEM)
     vector = pl.BlockSpec(memory_space=pltpu.VMEM)
     dma = pltpu.SemaphoreType.DMA
     updated, production = pl.pallas_call(
@@ -435,7 +456,7 @@
             pltpu.VMEM((NTR, CD), F32),
             pltpu.VMEM((COLS,), F32),
         ),
-        in_specs=[anywhere, scalars, scalars] + [anywhere] * 8,
+        in_specs=[anywhere] * 11,
         out_specs=(vector, vector),
         scratch_shapes=[
             pltpu.VMEM((NTR, CD), F32),
@@ -463,6 +484,8 @@
             pltpu.VMEM((NZ, 8, COLS), F32),
             pltpu.VMEM((8, COLS), F32),
             pltpu.VMEM((ny, 8, COLS), F32),
+            pltpu.SMEM((NT,), jnp.int32),
+            pltpu.SMEM((NT,), jnp.int32),
             pltpu.SMEM((NT,), jnp.int32),
             pltpu.SMEM((NT,), jnp.int32),
             pltpu.SMEM((2, BPD), jnp.int32),
@@ -497,7 +520,18 @@
         graze_preference,
         graze_maximum.reshape(1, PLK),
     )
-    return updated, production
+    return pl.pallas_call(
+        write_out,
+        out_shape=(
+            jax.ShapeDtypeStruct((NTR, CD), F32),
+            jax.ShapeDtypeStruct((COLS,), F32),
+        ),
+        in_specs=(vector, vector),
+        out_specs=(anywhere, anywhere),
+        scratch_shapes=[dma((2,))],
+        compiler_params=pltpu.CompilerParams(vmem_limit_bytes=1024 * 1024),
+        name="write_out",
+    )(updated, production)
 
 
 def solution(mesh):

time: 36.7 us -> 35.5 us (0.967)
  local copies, waits for them, and re-layouts: 1.66 us -> 0 us
    unnamed x2 -> x0, local copies, waits for them, and re-layouts: 1.66 us -> none
    pallas_call x0 -> x1, Pallas kernels: none -> 1.16 us  [per_device(): pl.pallas_call(write_out, out_shape=(jax.ShapeDtypeStruct((NTR, CD), F32)...]
    pallas_call x1, Pallas kernels: 34.3 us -> 33.3 us  [per_device(): pl.pallas_call(functools.partial(kernel, n_grp, n_dev), out_shape=(pltpu....]
where the time goes in v3:
time: 35.5 us; the launch traced here: 35.1 us
  Pallas kernels  34.5 us (97%)
  between operations  0.64 us (2%)
    pallas_call x1, Pallas kernels, per_device(): pl.pallas_call(functools.partial(kernel, n_grp, n_dev), out_shape=(pltpu....  33.3 us
    pallas_call x1, Pallas kernels, per_device(): pl.pallas_call(write_out, out_shape=(jax.ShapeDtypeStruct((NTR, CD), F32)...  1.16 us

profile of v3, /device:TPU:2, one launch (start us, length us, event | category | flops | bytes accessed | tf_op | source)
XLA Modules:
  0.0 35.1 jit_solution(2064969135651915405)
XLA Ops:
  0.6 33.3 %plankton_step.1 = (f32[96,4096]{1,0:T(8,128)S(1)}, f32[128]{0:T(128)S(1)}) custom-call(f32[96,4096]{1,0:T(8,128)} %tracer.1, s32[160]{0:T(256)} %rows_in.1, s32[160]{0:T(256)} %cols_in.1, bf16[160,128,128]{2,1,0:T(8,128)(2,1)} %tiles.1, s32[1,128]{1,0:T(1,128)} %bitcast.7, s32[1,128]{1,0:T(1,128)} %bitcast.8, f32[1,16]{1,0:T(1,128)} %bitcast.9, ...), custom_call_target="tpu_custom_call" | custom-call | tf_op jit(solution)/shard_map/plankton_step/pallas_call | solution.py:453
  34.0 1.2 %write_out.1 = (f32[96,4096]{1,0:T(8,128)}, f32[128]{0:T(128)}) custom-call(f32[96,4096]{1,0:T(8,128)S(1)} %get-tuple-element.4.updated, f32[128]{0:T(128)S(1)} %get-tuple-element.5.production), custom_call_target="tpu_custom_call" | custom-call | tf_op jit(solution)/shard_map/write_out/pallas_call | solution.py:523

commit v4 on v3

--- a/solution.py
+++ b/solution.py
@@ -137,6 +137,7 @@
     y_recv,
 ):
     ny = n_dev // NZ
+    share = COLS // n_dev
     grp = lax.axis_index("grp")
     dev = lax.axis_index("dev")
     me_y = dev // NZ
@@ -225,13 +226,13 @@
 
     for copy in spill[0:1]:
         copy.start()
-    for copy in index_copies:
-        copy.start()
     load.wait()
     round_blocks(0, REACH)
     halo[0].start()
     round_blocks(REACH, BPD - REACH)
     halo[1].start()
+    for copy in index_copies:
+        copy.start()
 
     for copy in small:
         copy.wait()
@@ -307,17 +308,16 @@
     gather_columns = ((lane_row >> 5) == (lane_col & 3)).astype(BF16)
     by_block = matmul(summed, gather_columns)
     column_sum = jnp.sum(jnp.where(pick_row, by_block, 0.0), axis=0, keepdims=True)
-    slot = iota((8 * NZ, COLS), 0)
-    slot_owner = (slot & 7) * NZ + (slot >> 3)
-    mine = (slot_owner == owner_v[...]) & ((slot & 7) < ny)
-    mine_f = mine.astype(F32)
+    owners = owner_v[...]
+    mine = (iota((n_dev, COLS), 0) == owners).astype(F32)
     earlier = (iota((COLS, COLS), 0) < iota((COLS, COLS), 1)).astype(BF16)
-    seen = matmul(mine_f.astype(BF16), earlier)
-    rank = jnp.sum(mine_f * seen, axis=0, keepdims=True)
-    target = rank + (dev * (COLS // n_dev)).astype(F32)
+    seen = matmul(mine.astype(BF16), earlier)
+    rank = jnp.sum(mine * seen, axis=0, keepdims=True)
+    target = rank + ((owners >> 3) * share + me_z * (ny * share)).astype(F32)
     put = (iota((COLS, COLS), 0).astype(F32) == target).astype(BF16)
-    sums = jnp.concatenate(split3(jnp.where(mine, column_sum, 0.0)), axis=1)
-    to_z[...] = matmul_nt(sums, jnp.concatenate([put, put, put], axis=1)).reshape(NZ, 8, COLS)
+    to_this_z = (owners & (NZ - 1)) == iota((NZ, COLS), 0)
+    sums = jnp.concatenate(split3(jnp.where(to_this_z, column_sum, 0.0)), axis=1)
+    to_z[...] = matmul_nt(sums, jnp.concatenate([put, put, put], axis=1)).reshape(NZ, 1, COLS)
     from_z[me_z] = to_z[me_z]
     z_copies = [
         remote(to_z.at[lax.rem(me_z + k, NZ)], from_z.at[me_z], z_send.at[k], z_recv.at[k], z_peers[k - 1])
@@ -413,11 +413,12 @@
 
     for copy in y_copies:
         copy.wait()
-    over_y = from_y[0]
-    for k in range(1, ny):
-        over_y += from_y[k]
-    in_row = iota((8, COLS), 0) == me_y
-    production[...] = jnp.sum(jnp.where(in_row, over_y, 0.0), axis=0)
+    rows = jnp.concatenate([from_y[k] for k in range(ny)] + [jnp.zeros((8 - ny, COLS), F32)], axis=0)
+    out_row, out_lane = iota((3 * COLS, COLS), 0) & (COLS - 1), iota((3 * COLS, COLS), 1)
+    source = ((out_lane // share) & (NZ - 1)) * (ny * share) + me_y * share + (out_lane & (share - 1))
+    moved = matmul(jnp.concatenate(split3(rows), axis=1), (out_row == source).astype(BF16))
+    from_row = iota((8, COLS), 1) // (NZ * share) == iota((8, COLS), 0)
+    production[...] = jnp.sum(jnp.where(from_row, moved, 0.0), axis=0)
 
 
 def write_out(updated, production, updated_out, production_out, sem):
@@ -480,10 +481,10 @@
             pltpu.VMEM((PLK, 3 * PLK), BF16),
             pltpu.VMEM((PLK, 3 * PLK), BF16),
             pltpu.VMEM((NUT, 3 * PLK), BF16),
-            pltpu.VMEM((NZ, 8, COLS), F32),
-            pltpu.VMEM((NZ, 8, COLS), F32),
-            pltpu.VMEM((8, COLS), F32),
-            pltpu.VMEM((ny, 8, COLS), F32),
+            pltpu.VMEM((NZ, 1, COLS), F32),
+            pltpu.VMEM((NZ, 1, COLS), F32),
+            pltpu.VMEM((1, COLS), F32),
+            pltpu.VMEM((ny, 1, COLS), F32),
             pltpu.SMEM((NT,), jnp.int32),
             pltpu.SMEM((NT,), jnp.int32),
             pltpu.SMEM((NT,), jnp.int32),

time: 35.5 us -> 34.8 us (0.980)
  Pallas kernels: 34.5 us -> 34 us
    pallas_call x1, Pallas kernels: 33.3 us -> 32.9 us  [per_device(): pl.pallas_call(functools.partial(kernel, n_grp, n_dev), out_shape=(pltpu....]
where the time goes in v4:
time: 34.8 us; the launch traced here: 34.7 us
  Pallas kernels  34 us (98%)
  between operations  0.64 us (2%)
    pallas_call x1, Pallas kernels, per_device(): pl.pallas_call(functools.partial(kernel, n_grp, n_dev), out_shape=(pltpu....  32.9 us
    pallas_call x1, Pallas kernels, per_device(): pl.pallas_call(write_out, out_shape=(jax.ShapeDtypeStruct((NTR, CD), F32)...  1.16 us

profile of v4, /device:TPU:2, one launch (start us, length us, event | category | flops | bytes accessed | tf_op | source)
XLA Modules:
  0.0 34.7 jit_solution(13833892876580242416)
XLA Ops:
  0.6 32.9 %plankton_step.1 = (f32[96,4096]{1,0:T(8,128)S(1)}, f32[128]{0:T(128)S(1)}) custom-call(f32[96,4096]{1,0:T(8,128)} %tracer.1, s32[160]{0:T(256)} %rows_in.1, s32[160]{0:T(256)} %cols_in.1, bf16[160,128,128]{2,1,0:T(8,128)(2,1)} %tiles.1, s32[1,128]{1,0:T(1,128)} %bitcast.7, s32[1,128]{1,0:T(1,128)} %bitcast.8, f32[1,16]{1,0:T(1,128)} %bitcast.9, ...), custom_call_target="tpu_custom_call" | custom-call | tf_op jit(solution)/shard_map/plankton_step/pallas_call | solution.py:454
  33.5 1.2 %write_out.1 = (f32[96,4096]{1,0:T(8,128)}, f32[128]{0:T(128)}) custom-call(f32[96,4096]{1,0:T(8,128)S(1)} %get-tuple-element.4.updated, f32[128]{0:T(128)S(1)} %get-tuple-element.5.production), custom_call_target="tpu_custom_call" | custom-call | tf_op jit(solution)/shard_map/write_out/pallas_call | solution.py:524

commit v5 on v4

--- a/solution.py
+++ b/solution.py
@@ -30,8 +30,9 @@
 REMINERAL = 0.2
 TIMESTEP = 0.5
 
-TILE_CHUNKS = 5
-TILES_SENT = SPILL // TILE_CHUNKS
+BOUNDS = (0, 4, 12, 17, 19)
+RELAYED = 1
+TILE_CHUNKS = len(BOUNDS) - 1
 GROUP = 256
 UNROLL = 8
 SMALL = 9
@@ -135,6 +136,9 @@
     z_recv,
     y_send,
     y_recv,
+    passing,
+    hop_send,
+    hop_recv,
 ):
     ny = n_dev // NZ
     share = COLS // n_dev
@@ -151,8 +155,13 @@
     z_peers = [(grp, me_y * NZ + lax.rem(me_z + k, NZ)) for k in range(1, NZ)]
     y_peers = [(grp, lax.rem(me_y + k, ny) * NZ + me_z) for k in range(1, ny)]
 
+    third = (grp, me_y * NZ + lax.rem(me_z + 3, NZ))
+    origin = me_y * NZ + lax.rem(me_z + 2, NZ)
+    last_to = (grp, lax.rem(origin + n_dev - 1, n_dev))
+    sender = lax.rem(dev + 1, n_dev)
+    last_from = (grp, (sender // NZ) * NZ + lax.rem(lax.rem(sender, NZ) + NZ - 2, NZ))
     barrier = pltpu.get_barrier_semaphore()
-    for peer in [left, right] + z_peers + y_peers:
+    for peer in [left, right, last_from] + z_peers + y_peers:
         pl.semaphore_signal(barrier, inc=1, device_id=peer, device_id_type=MESH)
 
     load = pltpu.make_async_copy(tracer, tr, tracer_sem)
@@ -178,7 +187,7 @@
     load_tiles = pltpu.make_async_copy(tiles, own_tiles, tiles_sem)
     load_tiles.start()
 
-    pl.semaphore_wait(barrier, 2 + (NZ - 1) + (ny - 1))
+    pl.semaphore_wait(barrier, 3 + (NZ - 1) + (ny - 1))
 
     def remote(source, target, send, recv, peer):
         return pltpu.make_async_remote_copy(
@@ -212,8 +221,8 @@
     ]
     spill = [
         remote(
-            (own_tiles if c else tiles).at[pl.ds(c * TILES_SENT, TILES_SENT)],
-            got_tiles.at[pl.ds(c * TILES_SENT, TILES_SENT)],
+            (own_tiles if c else tiles).at[pl.ds(BOUNDS[c], BOUNDS[c + 1] - BOUNDS[c])],
+            got_tiles.at[pl.ds(BOUNDS[c], BOUNDS[c + 1] - BOUNDS[c])],
             spill_send.at[c],
             spill_recv.at[c],
             left,
@@ -224,6 +233,13 @@
         for b in range(first, first + blocks):
             ext[REACH + b] = tr[:, b * BLK : (b + 1) * BLK].astype(BF16)
 
+    relayed = pl.ds(SPILL - RELAYED, RELAYED)
+    hops = [
+        remote(tiles.at[relayed], passing.at[0], hop_send.at[0], hop_recv.at[0], third),
+        remote(passing.at[0], passing.at[1], hop_send.at[1], hop_recv.at[1], third),
+        remote(passing.at[1], got_tiles.at[relayed], hop_send.at[2], hop_recv.at[2], last_to),
+    ]
+    hops[0].start()
     for copy in spill[0:1]:
         copy.start()
     load.wait()
@@ -327,7 +343,9 @@
         copy.start()
 
     load_tiles.wait()
-    for copy in spill[1:3]:
+    hops[0].wait()
+    hops[1].start()
+    for copy in spill[1:2]:
         copy.start()
     first_row = position * BPD
 
@@ -388,7 +406,9 @@
     for copy in y_copies:
         copy.start()
 
-    for copy in spill[3:]:
+    hops[1].wait()
+    hops[2].start()
+    for copy in spill[2:]:
         copy.start()
 
     lax.fori_loop(80, NT, own, run, unroll=UNROLL)
@@ -398,9 +418,9 @@
         updated[:, lanes] += jnp.where(place[1, r] == 1, runs[place[0, r]], 0.0)
 
     run = jnp.zeros((NTR, BLK), F32)
-    for c in range(TILE_CHUNKS):
-        spill[c].wait()
-        for s in range(c * TILES_SENT, (c + 1) * TILES_SENT):
+    for c in range(TILE_CHUNKS + 1):
+        (spill + hops[2:])[c].wait()
+        for s in range(*(BOUNDS + (SPILL,))[c : c + 2]):
             block = jnp.clip(got_cols[s] - first_col, 0, BPD + 2 * REACH - 1)
             term = matmul_nt(ext[block], got_tiles[s])
             goes_on = got_rows[s] == got_rows[max(s - 1, 0)]
@@ -503,6 +523,9 @@
             dma((NZ,)),
             dma((ny,)),
             dma((ny,)),
+            pltpu.VMEM((2, RELAYED, BLK, BLK), BF16),
+            dma((3,)),
+            dma((3,)),
         ],
         compiler_params=pltpu.CompilerParams(
             collective_id=0, has_side_effects=True, vmem_limit_bytes=56 * 1024 * 1024

time: 34.8 us -> 34.4 us (0.989)
  Pallas kernels: 34 us -> 33.6 us
    pallas_call x1, Pallas kernels: 32.9 us -> 32.4 us  [per_device(): pl.pallas_call(functools.partial(kernel, n_grp, n_dev), out_shape=(pltpu....]
where the time goes in v5:
time: 34.4 us; the launch traced here: 34.2 us
  Pallas kernels  33.6 us (98%)
  between operations  0.64 us (2%)
    pallas_call x1, Pallas kernels, per_device(): pl.pallas_call(functools.partial(kernel, n_grp, n_dev), out_shape=(pltpu....  32.4 us
    pallas_call x1, Pallas kernels, per_device(): pl.pallas_call(write_out, out_shape=(jax.ShapeDtypeStruct((NTR, CD), F32)...  1.16 us

profile of v5, /device:TPU:2, one launch (start us, length us, event | category | flops | bytes accessed | tf_op | source)
XLA Modules:
  0.0 34.2 jit_solution(14683710314523634428)
XLA Ops:
  0.6 32.4 %plankton_step.1 = (f32[96,4096]{1,0:T(8,128)S(1)}, f32[128]{0:T(128)S(1)}) custom-call(f32[96,4096]{1,0:T(8,128)} %tracer.1, s32[160]{0:T(256)} %rows_in.1, s32[160]{0:T(256)} %cols_in.1, bf16[160,128,128]{2,1,0:T(8,128)(2,1)} %tiles.1, s32[1,128]{1,0:T(1,128)} %bitcast.7, s32[1,128]{1,0:T(1,128)} %bitcast.8, f32[1,16]{1,0:T(1,128)} %bitcast.9, ...), custom_call_target="tpu_custom_call" | custom-call | tf_op jit(solution)/shard_map/plankton_step/pallas_call | solution.py:474
  33.0 1.2 %write_out.1 = (f32[96,4096]{1,0:T(8,128)}, f32[128]{0:T(128)}) custom-call(f32[96,4096]{1,0:T(8,128)S(1)} %get-tuple-element.4.updated, f32[128]{0:T(128)S(1)} %get-tuple-element.5.production), custom_call_target="tpu_custom_call" | custom-call | tf_op jit(solution)/shard_map/write_out/pallas_call | solution.py:547
